TPU v7x, 256 devices: a whole 4x4x8 slice. The times are simulated.
256 devices in a mesh: hid: 16 (over z, x_hi), wid: 16 (over y, x_lo, core).
Axes of the slice: x: 4 (x_hi: 2, x_lo: 2; x = x_hi * 2 + x_lo), y: 4, z: 8, core: 2. Of those that a mesh axis runs over, the one named last changes fastest.
Arguments:
- tokens: bfloat16 [1024, 8192], P('hid', 'wid'), may hold values from -6 to 6
- grad_out: bfloat16 [1024, 8192], P('hid', 'wid'), may hold values from -6 to 6
- gate_codes: bfloat16 [8192, 14336], P('wid', 'hid'), may hold values from -7.5 to 7.5, as said below
- gate_scale: float32 [64, 112], P('wid', 'hid'), may hold values from 0.0022097088 to 0.008838835
- up_codes: bfloat16 [8192, 14336], P('wid', 'hid'), may hold values from -7.5 to 7.5, as said below
- up_scale: float32 [64, 112], P('wid', 'hid'), may hold values from 0.0022097088 to 0.008838835
- down_codes: bfloat16 [14336, 8192], P('hid', 'wid'), may hold values from -7.5 to 7.5, as said below
- down_scale: float32 [112, 64], P('hid', 'wid'), may hold values from 0.0016703828 to 0.006681531
Outputs:
- grad_tokens: bfloat16 [1024, 8192], P('hid', 'wid')
- grad_gate: bfloat16 [8192, 14336], P('wid', 'hid')
- grad_up: bfloat16 [8192, 14336], P('wid', 'hid')
- grad_down: bfloat16 [14336, 8192], P('hid', 'wid')
- block_norms: float32 [3, 64, 112], P(None, 'wid', 'hid')
Inputs may be any that keep to these rules, and one draw needn't show every extreme that they name: Every entry of gate_codes is an e4m3 value: a sign times 2 to a power from -2 to 2 times 1 + m / 8 with m from 0 to 7. Every entry of up_codes is an e4m3 value of the same kind. Every entry of down_codes is an e4m3 value of the same kind.
All inputs are finite; a program needn't handle non-finite values.
Results may differ from a plain program's by a relative error of at most 0.039.
Values may be sent and summed in bfloat16 or wider, within the bound.
A program may use at most 64 MiB of HBM per device.

v0:
```python
import jax
import jax.numpy as jnp
from jax import lax
from jax.sharding import PartitionSpec as P

BLK = 128


def dequant(codes, scales):
    expanded = jnp.repeat(jnp.repeat(scales, BLK, axis=0), BLK, axis=1)
    return (codes.astype(jnp.float32) * expanded).astype(jnp.bfloat16)


def block_squares(matrix):
    rows, cols = matrix.shape
    blocks = matrix.reshape(rows // BLK, BLK, cols // BLK, BLK)
    return jnp.sum(blocks * blocks, axis=(1, 3))


def contract_rows(left, right):
    return lax.dot_general(
        left, right, (((0,), (0,)), ((), ())), preferred_element_type=jnp.float32
    )


def contract_cols(left, right):
    return lax.dot_general(
        left, right, (((1,), (1,)), ((), ())), preferred_element_type=jnp.float32
    )


def nonlinear(gate, upper, grad_hidden):
    sigma = jax.nn.sigmoid(gate)
    active = gate * sigma
    hidden = (active * upper).astype(jnp.bfloat16)
    d_gate = (grad_hidden * upper * sigma * (1.0 + gate * (1.0 - sigma))).astype(jnp.bfloat16)
    d_up = (grad_hidden * active).astype(jnp.bfloat16)
    return (hidden, d_gate, d_up)


def body(tokens, grad_out, gate_codes, gate_scale, up_codes, up_scale, down_codes, down_scale):
    gate_weight = dequant(gate_codes, gate_scale)
    up_weight = dequant(up_codes, up_scale)
    down_weight = dequant(down_codes, down_scale)
    all_tokens, all_grads = (
        lax.all_gather(tokens, "hid", axis=0, tiled=True),
        lax.all_gather(grad_out, "hid", axis=0, tiled=True),
    )
    gate_part = jnp.dot(all_tokens, gate_weight, preferred_element_type=jnp.float32)
    up_part = jnp.dot(all_tokens, up_weight, preferred_element_type=jnp.float32)
    grad_part = contract_cols(all_grads, down_weight)
    gate_sum, up_sum, grad_sum = (
        lax.psum_scatter(
            gate_part.astype(jnp.bfloat16), "wid", scatter_dimension=0, tiled=True
        ).astype(jnp.float32),
        lax.psum_scatter(
            up_part.astype(jnp.bfloat16), "wid", scatter_dimension=0, tiled=True
        ).astype(jnp.float32),
        lax.psum_scatter(
            grad_part.astype(jnp.bfloat16), "wid", scatter_dimension=0, tiled=True
        ).astype(jnp.float32),
    )
    own_hidden, own_dgate, own_dup = nonlinear(gate_sum, up_sum, grad_sum)
    hidden, d_gate, d_up = (
        lax.all_gather(own_hidden, "wid", axis=0, tiled=True),
        lax.all_gather(own_dgate, "wid", axis=0, tiled=True),
        lax.all_gather(own_dup, "wid", axis=0, tiled=True),
    )
    local_term = contract_cols(d_gate, gate_weight) + contract_cols(d_up, up_weight)
    grad_sum_tokens = lax.psum_scatter(
        local_term.astype(jnp.bfloat16), "hid", scatter_dimension=0, tiled=True
    )
    full_gate = contract_rows(all_tokens, d_gate)
    full_up = contract_rows(all_tokens, d_up)
    full_down = contract_rows(hidden, all_grads)
    block_norms = jnp.stack(
        [block_squares(full_gate), block_squares(full_up), block_squares(full_down).T]
    )
    return (
        grad_sum_tokens,
        full_gate.astype(jnp.bfloat16),
        full_up.astype(jnp.bfloat16),
        full_down.astype(jnp.bfloat16),
        block_norms,
    )


def solution(mesh):
    in_specs = (
        P("hid", "wid"),
        P("hid", "wid"),
        P("wid", "hid"),
        P("wid", "hid"),
        P("wid", "hid"),
        P("wid", "hid"),
        P("hid", "wid"),
        P("hid", "wid"),
    )
    out_specs = (
        P("hid", "wid"),
        P("wid", "hid"),
        P("wid", "hid"),
        P("hid", "wid"),
        P(None, "wid", "hid"),
    )
    return jax.shard_map(body, mesh=mesh, in_specs=in_specs, out_specs=out_specs, check_vma=False)
```

profile of v0, /device:TPU:1, one launch (start us, length us, event | category | flops | bytes accessed | tf_op | source)
XLA Modules:
  0.0 694.4 jit_solution(9325887190689432085)
XLA Ops:
  8.7 1.5 copy.38
  10.5 79.0 %all-gather.8.cloned.1.call-done = bf16[1024,512]{1,0:T(8,128)(2,1)} async-done(((bf16[64,512]{1,0:T(8,128)(2,1)}), bf16[1024,512]{1,0:T(8,128)(2,1)}) %all-gather.8.cloned.1.call-update) | async-done | bytes 1048592 | tf_op jit(solution)/shard_map/all_gather | solution.py:46
  89.5 2.4 convert_bitcast_fusion.1
  91.9 2.5 copy.51
  98.5 2.5 copy.53
  101.8 65.7 %all-gather.6.cloned.1.call-done = bf16[1024,512]{1,0:T(8,128)(2,1)} async-done(((bf16[64,512]{1,0:T(8,128)(2,1)}), bf16[1024,512]{1,0:T(8,128)(2,1)}) %all-gather.6.cloned.1.call-update) | async-done | bytes 1048592 | tf_op jit(solution)/shard_map/all_gather | solution.py:47
  168.7 2.3 convert_bitcast_fusion.2
  171.1 2.5 copy.49
  173.6 59.3 %reduce-scatter.15.cloned.1.call-done = bf16[64,896]{1,0:T(8,128)(2,1)} async-done(((bf16[1024,896]{1,0:T(8,128)(2,1)}), bf16[64,896]{1,0:T(8,128)(2,1)}) %reduce-scatter.15.cloned.1.call-update) | async-done | bytes 114704 | tf_op jit(solution)/shard_map/reduce_scatter | solution.py:56
  233.0 67.0 %reduce-scatter.17.cloned.1.call-done = bf16[64,896]{1,0:T(8,128)(2,1)} async-done(((bf16[1024,896]{1,0:T(8,128)(2,1)}), bf16[64,896]{1,0:T(8,128)(2,1)}) %reduce-scatter.17.cloned.1.call-update) | async-done | bytes 114704 | tf_op jit(solution)/shard_map/reduce_scatter | solution.py:53
  300.0 68.0 %reduce-scatter.13.cloned.1.call-done = bf16[64,896]{1,0:T(8,128)(2,1)} async-done(((bf16[1024,896]{1,0:T(8,128)(2,1)}), bf16[64,896]{1,0:T(8,128)(2,1)}) %reduce-scatter.13.cloned.1.call-update) | async-done | bytes 114704 | tf_op jit(solution)/shard_map/reduce_scatter | solution.py:59
  368.0 1.9 fusion.8
  371.6 37.4 %all-gather.10.cloned.1.call-done = bf16[1024,896]{1,0:T(8,128)(2,1)} async-done(((bf16[64,896]{1,0:T(8,128)(2,1)}), bf16[1024,896]{1,0:T(8,128)(2,1)}) %all-gather.10.cloned.1.call-update) | async-done | bytes 1835024 | tf_op jit(solution)/shard_map/all_gather | solution.py:66
  408.9 4.1 fusion.14
  413.0 34.2 %all-gather.12.cloned.1.call-done = bf16[1024,896]{1,0:T(8,128)(2,1)} async-done(((bf16[64,896]{1,0:T(8,128)(2,1)}), bf16[1024,896]{1,0:T(8,128)(2,1)}) %all-gather.12.cloned.1.call-update) | async-done | bytes 1835024 | tf_op jit(solution)/shard_map/all_gather | solution.py:67
  447.2 4.4 add_convert_fusion
  451.6 4.2 multiply_bitcast_fusion.1
  457.1 4.2 multiply_bitcast_fusion
  462.5 22.9 %all-gather.14.cloned.1.call-done = bf16[1024,896]{1,0:T(8,128)(2,1)} async-done(((bf16[64,896]{1,0:T(8,128)(2,1)}), bf16[1024,896]{1,0:T(8,128)(2,1)}) %all-gather.14.cloned.1.call-update) | async-done | bytes 1835024 | tf_op jit(solution)/shard_map/all_gather | solution.py:65
  485.4 4.2 fusion.13
  489.6 1.9 mul.71
  492.0 1.9 mul.69
  494.4 1.9 mul.66
  497.3 190.6 %reduce-scatter.11.cloned.1.call-done = bf16[64,512]{1,0:T(8,128)(2,1)} async-done(((bf16[1024,512]{1,0:T(8,128)(2,1)}), bf16[64,512]{1,0:T(8,128)(2,1)}) %reduce-scatter.11.cloned.1.call-update) | async-done | bytes 65552 | tf_op jit(solution)/shard_map/reduce_scatter | solution.py:70
  (60 shorter events, 14.3 us)
Async XLA Ops:
  7.2 3.0 copy-start.6
  7.2 82.3 %all-gather.8.cloned.1.call-start = ((), (), s32[]{:S(2)}) async-start(), calls=%async_computation.5 | async-start | bytes 1114112 | tf_op jit(solution)/shard_map/all_gather | solution.py:46
  7.9 159.6 %all-gather.6.cloned.1.call-start = ((), (), s32[]{:S(2)}) async-start(), calls=%async_computation.4 | async-start | bytes 1114112 | tf_op jit(solution)/shard_map/all_gather | solution.py:47
  8.7 224.3 %reduce-scatter.15.cloned.1.call-start = ((), (), s32[]{:S(2)}) async-start(), calls=%async_computation.11 | async-start | bytes 1949696 | tf_op jit(solution)/shard_map/reduce_scatter | solution.py:56
  10.5 81.3 %copy-start.2 = (bf16[512,896]{0,1:T(8,128)(2,1)}, bf16[512,896]{0,1:T(8,128)(2,1)S(1)}, u32[]{:S(2)}) copy-start(bf16[512,896]{0,1:T(8,128)(2,1)S(1)} %fusion.2) | copy-start | bytes 2752516
  94.4 1.2 copy-start.1
  94.4 1.7 copy-start.7
  94.4 3.0 copy-start.9
  94.4 205.6 %reduce-scatter.17.cloned.1.call-start = ((), (), s32[]{:S(2)}) async-start(), calls=%async_computation.12 | async-start | bytes 1949696 | tf_op jit(solution)/shard_map/reduce_scatter | solution.py:53
  96.5 0.9 copy-start.4
  101.0 0.7 copy-start.8
  101.0 266.9 %reduce-scatter.13.cloned.1.call-start = ((), (), s32[]{:S(2)}) async-start(), calls=%async_computation.10 | async-start | bytes 1949696 | tf_op jit(solution)/shard_map/reduce_scatter | solution.py:59
  167.5 1.2 copy-start
  173.6 235.4 %copy-start.5 = (bf16[512,896]{0,1:T(8,128)(2,1)S(1)}, bf16[512,896]{0,1:T(8,128)(2,1)}, u32[]{:S(2)}) copy-start(bf16[512,896]{0,1:T(8,128)(2,1)} %copy-done.4) | copy-start | bytes 2752516
  173.6 235.3 %all-gather.10.cloned.1.call-start = ((), (), s32[]{:S(2)}) async-start(), calls=%async_computation.6 | async-start | bytes 1949696 | tf_op jit(solution)/shard_map/all_gather | solution.py:66
  369.9 77.3 %all-gather.12.cloned.1.call-start = ((), (), s32[]{:S(2)}) async-start(), calls=%async_computation.7 | async-start | bytes 1949696 | tf_op jit(solution)/shard_map/all_gather | solution.py:67
  370.6 114.8 %all-gather.14.cloned.1.call-start = ((), (), s32[]{:S(2)}) async-start(), calls=%async_computation.9 | async-start | bytes 1949696 | tf_op jit(solution)/shard_map/all_gather | solution.py:65
  371.4 75.8 %copy-start.3 = (bf16[512,896]{0,1:T(8,128)(2,1)S(1)}, bf16[512,896]{0,1:T(8,128)(2,1)}, u32[]{:S(2)}) copy-start(bf16[512,896]{0,1:T(8,128)(2,1)} %copy-done.2) | copy-start | bytes 2752516
  371.4 316.5 %reduce-scatter.11.cloned.1.call-start = ((), (), s32[]{:S(2)}) async-start(), calls=%async_computation.8 | async-start | bytes 1114112 | tf_op jit(solution)/shard_map/reduce_scatter | solution.py:70
Sparse Core Ops, SparseCore 0:
  10.6 78.8 all-gather.7
  92.1 75.3 all-gather.5
  170.1 62.8 reduce-scatter.14
  235.6 64.4 reduce-scatter.16
  302.4 65.5 reduce-scatter.12
  370.4 38.5 all-gather.9
  410.9 36.1 all-gather.11
  449.2 36.1 all-gather.13
  490.3 197.5 reduce-scatter.10
where the time goes:
time: 699 us; the launch traced here: 694 us
  waiting for transfers between devices  627 us (90%)
  matrix products  26.9 us (4%)
  local copies, waits for them, and re-layouts  22.2 us (3%)
  between operations  14 us (2%)
    reduce_scatter x1, waiting for transfers between devices, body(): lax.psum_scatter(local_term.astype(jnp.bfloat16), 'hid', scatter_dimensio...  191 us
    all_gather x1, waiting for transfers between devices, body(): lax.all_gather(tokens, 'hid', axis=0, tiled=True)  79 us
    reduce_scatter x1, waiting for transfers between devices, body(): lax.psum_scatter(grad_part.astype(jnp.bfloat16), 'wid', scatter_dimension...  68 us
    reduce_scatter x1, waiting for transfers between devices, body(): lax.psum_scatter(gate_part.astype(jnp.bfloat16), 'wid', scatter_dimension...  67 us
    all_gather x1, waiting for transfers between devices, body(): lax.all_gather(grad_out, 'hid', axis=0, tiled=True)  65.7 us
    reduce_scatter x1, waiting for transfers between devices, body(): lax.psum_scatter(up_part.astype(jnp.bfloat16), 'wid', scatter_dimension=0...  59.3 us
    all_gather x1, waiting for transfers between devices, body(): lax.all_gather(own_dgate, 'wid', axis=0, tiled=True)  37.4 us
    all_gather x1, waiting for transfers between devices, body(): lax.all_gather(own_dup, 'wid', axis=0, tiled=True)  34.2 us
  transfers between devices with their start and end apart: 9, of which 9 were waited for; matrix products, arithmetic and copies ran while one was open for 7% of the time, Pallas kernels for 0%

commit v1 on v0

v1 whole, which is shorter than its diff:
```python
import functools

import jax
import jax.numpy as jnp
from jax import lax
from jax.experimental import pallas as pl
from jax.experimental.pallas import tpu as pltpu
from jax.sharding import PartitionSpec as P

BLK = 128
NZ = 8
CHUNKS = ((1, 7), (2, 6), (3, 5), (0, 4))
POS = {r: (c, h) for c, pair in enumerate(CHUNKS) for h, r in enumerate(pair)}
NC = len(CHUNKS)
ROWS = 16
ORDER = ((0, 1, 2), (1, 2, 0), (2, 0, 1))
BF = jnp.bfloat16
F32 = jnp.float32


def matmul(left, right, dims=((1,), (0,))):
    return lax.dot_general(left, right, (dims, ((), ())), preferred_element_type=F32)


def kernel(
    tok_in, gro_in, gc_in, gs, uc_in, us, dc_in, ds,
    gt_out, gg_out, gu_out, gd_out, bn_out,
    X, codes_g, codes_u, codes_d, wg, wu, wd, part, rb0, rb1, rb2, rb3, ag, term, zrecv, xsend, xrecv,
    st_g, st_u, st_d, st_t,
    loc_sem, own_sem, xs_sem, ring_s, ring_r, wid_s, wid_r, z_s, z_r, xf_sem, out_sem,
):
    hid, wid = lax.axis_index("hid"), lax.axis_index("wid")
    z, xhi = hid // 2, hid % 2
    y, xlo, core = wid // 4, (wid // 2) % 2, wid % 2
    bit_a, bit_b = (y + y // 2) % 2, y // 2
    bits = (xlo, bit_a, bit_b)
    core_peer = wid + 1 - 2 * core
    x_peer = (y * 2 + 1 - xlo) * 2 + core
    a_peer = ((y + 1 - 2 * (y % 2)) * 2 + xlo) * 2 + core
    b_peer = ((3 - y) * 2 + xlo) * 2 + core
    pair_peer = (x_peer, a_peer, b_peer)
    xhi_peer = z * 2 + 1 - xhi

    def z_peer(r):
        return ((z + r) % NZ) * 2 + xhi

    barrier = pltpu.get_barrier_semaphore()
    for peer in (core_peer,) + pair_peer:
        pl.semaphore_signal(barrier, inc=1, device_id={"wid": peer}, device_id_type=pl.DeviceIdType.MESH)
    for peer in [xhi_peer] + [z_peer(r) for r in range(1, NZ)]:
        pl.semaphore_signal(barrier, inc=1, device_id={"hid": peer}, device_id_type=pl.DeviceIdType.MESH)

    c0, h0 = POS[0]
    own = [
        pltpu.make_async_copy(tok_in, X.at[c0, 0, h0, 0], own_sem.at[0]),
        pltpu.make_async_copy(gro_in, X.at[c0, 1, h0, 0], own_sem.at[1]),
    ]
    loads = [
        pltpu.make_async_copy(gc_in, codes_g, loc_sem.at[0]),
        pltpu.make_async_copy(uc_in, codes_u, loc_sem.at[1]),
        pltpu.make_async_copy(dc_in, codes_d, loc_sem.at[2]),
    ]
    for copy in own + loads:
        copy.start()
    for copy in own:
        copy.wait()
    pl.semaphore_wait(barrier, 12)

    sends = []

    def remote(src, dst, send, recv, where):
        return pltpu.make_async_remote_copy(
            src_ref=src, dst_ref=dst, send_sem=send, recv_sem=recv,
            device_id=where, device_id_type=pl.DeviceIdType.MESH,
        )

    def go(copy):
        copy.start()
        sends.append(copy)

    x_copy = remote(X.at[c0, :, h0, 0], X.at[c0, :, h0, 1], xs_sem.at[0], xs_sem.at[1], {"hid": xhi_peer})
    ring = {}
    for way, sign in ((0, -1), (1, 1)):
        for j in range(1, 5):
            for xh in range(2):
                cs, hs = POS[(sign * (j - 1)) % NZ]
                cd, hd = POS[(sign * j) % NZ]
                kind = slice(None) if j < 4 else way
                ring[way, j, xh] = remote(
                    X.at[cs, kind, hs, xh], X.at[cd, kind, hd, xh],
                    ring_s.at[way, j - 1, xh], ring_r.at[way, j - 1, xh], {"hid": z_peer(-sign)},
                )

    def forward(j, xh):
        for way in range(2):
            ring[way, j, xh].wait_recv()
            if j < 4:
                go(ring[way, j + 1, xh])

    def dequant(codes, scales, weight):
        rows, cols = weight.shape
        for i in range(rows // BLK):
            for j in range(cols // BLK):
                at = (slice(i * BLK, (i + 1) * BLK), slice(j * BLK, (j + 1) * BLK))
                weight[at] = (codes[at].astype(F32) * scales[i, j]).astype(BF)

    go(x_copy)
    go(ring[0, 1, 0])
    go(ring[1, 1, 0])
    loads[0].wait()
    dequant(codes_g, gs, wg)
    forward(1, 0)
    x_copy.wait_recv()
    go(ring[0, 1, 1])
    go(ring[1, 1, 1])
    loads[1].wait()
    dequant(codes_u, us, wu)
    loads[2].wait()
    dequant(codes_d, ds, wd)
    forward(1, 1)

    def at_bits(free, other=None):
        index = []
        for d in range(3):
            if d in free:
                index.append(slice(None))
            elif d == other:
                index.append(1 - bits[d])
            else:
                index.append(bits[d])
        return tuple(index)

    def core_sum(c, k):
        return remote(part.at[c, k, 1 - core], rb0.at[c, k], wid_s.at[c, k, 0], wid_r.at[c, k, 0], {"wid": core_peer})

    def pair_sum(c, k, s):
        order = ORDER[k]
        index = at_bits(order[s:], order[s - 1])
        return remote(
            part.at[(c, k, core) + index], (rb1, rb2, rb3)[s - 1].at[c, k],
            wid_s.at[c, k, s], wid_r.at[c, k, s], {"wid": pair_peer[order[s - 1]]},
        )

    def pair_gather(c, k, s):
        order = ORDER[k]
        ref = ag.at[(c, k, core) + at_bits(order[s:])]
        return remote(ref, ref, wid_s.at[c, k, 7 - s], wid_r.at[c, k, 7 - s], {"wid": pair_peer[order[s - 1]]})

    def core_gather(c, k):
        ref = ag.at[c, k, core]
        return remote(ref, ref, wid_s.at[c, k, 7], wid_r.at[c, k, 7], {"wid": core_peer})

    def add_into(ref, other):
        ref[...] = (ref[...].astype(F32) + other[...].astype(F32)).astype(BF)

    def stage_partial(c):
        toks = X[c, 0].reshape(256, 512)
        part[c, 0] = matmul(toks, wg[...]).astype(BF).reshape(2, 2, 2, 2, ROWS, 896)
        go(core_sum(c, 0))
        part[c, 1] = matmul(toks, wu[...]).astype(BF).reshape(2, 2, 2, 2, ROWS, 896)
        go(core_sum(c, 1))
        grads = X[c, 1].reshape(256, 512)
        part[c, 2] = matmul(grads, wd[...], ((1,), (1,))).astype(BF).reshape(2, 2, 2, 2, ROWS, 896)
        go(core_sum(c, 2))

    def stage_core(c):
        for k in range(3):
            core_sum(c, k).wait_recv()
            add_into(part.at[c, k, core], rb0.at[c, k])
            go(pair_sum(c, k, 1))

    def stage_pair(c, s):
        for k in range(3):
            order = ORDER[k]
            pair_sum(c, k, s).wait_recv()
            add_into(part.at[(c, k, core) + at_bits(order[s:])], (rb1, rb2)[s - 1].at[c, k])
            go(pair_sum(c, k, s + 1))

    def stage_nonlinear(c):
        sums = []
        for k in range(3):
            pair_sum(c, k, 3).wait_recv()
            sums.append(part[(c, k, core) + bits].astype(F32) + rb3[c, k].astype(F32))
        gate, upper, grad = sums
        sigma = jax.nn.sigmoid(gate)
        active = gate * sigma
        ag[(c, 0, core) + bits] = (active * upper).astype(BF)
        go(pair_gather(c, 0, 3))
        ag[(c, 1, core) + bits] = (grad * upper * sigma * (1.0 + gate * (1.0 - sigma))).astype(BF)
        go(pair_gather(c, 1, 3))
        ag[(c, 2, core) + bits] = (grad * active).astype(BF)
        go(pair_gather(c, 2, 3))

    def stage_gather(c, s):
        for k in range(3):
            pair_gather(c, k, s).wait_recv()
            go(pair_gather(c, k, s - 1) if s > 1 else core_gather(c, k))

    def z_send(r):
        c, h = POS[r]
        back = (-r) % NZ
        return remote(term.at[c, h], zrecv.at[back], z_s.at[r], z_r.at[back], {"hid": z_peer(r)})

    def stage_term(c):
        for k in range(3):
            core_gather(c, k).wait_recv()
        total = matmul(ag[c, 1].reshape(256, 896), wg[...], ((1,), (1,)))
        total += matmul(ag[c, 2].reshape(256, 896), wu[...], ((1,), (1,)))
        term[c] = total.astype(BF).reshape(2, 128, 512)
        for r in CHUNKS[c]:
            if r:
                go(z_send(r))

    stages = [
        stage_partial,
        stage_core,
        lambda c: stage_pair(c, 1),
        lambda c: stage_pair(c, 2),
        stage_nonlinear,
        lambda c: stage_gather(c, 3),
        lambda c: stage_gather(c, 2),
        lambda c: stage_gather(c, 1),
        stage_term,
    ]
    forwards = [
        lambda: forward(2, 0),
        lambda: forward(2, 1),
        lambda: forward(3, 0),
        lambda: forward(3, 1),
        lambda: forward(4, 0),
        lambda: forward(4, 1),
    ]
    needs = (0, 2, 4, 6)
    done = 0
    stagger = 2
    for tick in range(len(stages) + stagger * (NC - 1)):
        for c in range(NC):
            step = tick - stagger * c
            if 0 <= step < len(stages):
                if step == 0:
                    while done < needs[c]:
                        forwards[done]()
                        done += 1
                stages[step](c)
        if done < len(forwards):
            forwards[done]()
            done += 1

    toks = X[:, 0].reshape(1024, 512)
    outs = []

    def block_sums(full):
        rows, cols = full.shape
        sums = jnp.sum((full * full).reshape(rows // BLK, BLK, cols), axis=1)
        of_block = (
            lax.broadcasted_iota(jnp.int32, (cols // BLK, cols), 1) // BLK
            == lax.broadcasted_iota(jnp.int32, (cols // BLK, cols), 0)
        ).astype(F32)
        return sums, of_block

    def exact(left, right):
        return lax.dot_general(
            left, right, (((1,), (1,)), ((), ())), precision=lax.Precision.HIGHEST, preferred_element_type=F32
        )

    def weight_grad(k, left, right, stage, out, flip):
        full = matmul(left, right, ((0,), (0,)))
        stage[...] = full.astype(BF)
        copy = pltpu.make_async_copy(stage, out, out_sem.at[k])
        copy.start()
        outs.append(copy)
        sums, of_block = block_sums(full)
        bn_out[k] = exact(of_block, sums) if flip else exact(sums, of_block)

    weight_grad(0, toks, ag[:, 1].reshape(1024, 896), st_g, gg_out, False)
    weight_grad(1, toks, ag[:, 2].reshape(1024, 896), st_u, gu_out, False)

    total = term[c0, h0].astype(F32)
    for r in (1, 7, 2, 6, 3, 5, 4):
        z_send((-r) % NZ).wait_recv()
        total += zrecv[r].astype(F32)
    xsend[...] = total[64:].astype(BF)
    last = remote(xsend, xrecv, xf_sem.at[0], xf_sem.at[1], {"hid": xhi_peer})
    go(last)
    weight_grad(2, ag[:, 0].reshape(1024, 896), X[:, 1].reshape(1024, 512), st_d, gd_out, True)
    last.wait_recv()
    st_t[...] = (total[:64] + xrecv[...].astype(F32)).astype(BF)
    copy = pltpu.make_async_copy(st_t, gt_out, out_sem.at[3])
    copy.start()
    outs.append(copy)
    for copy in outs:
        copy.wait()
    for copy in sends:
        copy.wait_send()


def body(tokens, grad_out, gate_codes, gate_scale, up_codes, up_scale, down_codes, down_scale):
    hbm = pl.BlockSpec(memory_space=pl.ANY)
    smem = pl.BlockSpec(memory_space=pltpu.SMEM)
    vmem = pl.BlockSpec(memory_space=pltpu.VMEM)
    dma = pltpu.SemaphoreType.DMA
    blocks = (ROWS, 896)
    return pl.pallas_call(
        kernel,
        out_shape=(
            jax.ShapeDtypeStruct((64, 512), BF),
            jax.ShapeDtypeStruct((512, 896), BF),
            jax.ShapeDtypeStruct((512, 896), BF),
            jax.ShapeDtypeStruct((896, 512), BF),
            jax.ShapeDtypeStruct((3, 4, 7), F32),
        ),
        in_specs=[hbm, hbm, hbm, smem, hbm, smem, hbm, smem],
        out_specs=(hbm, hbm, hbm, hbm, vmem),
        scratch_shapes=[
            pltpu.VMEM((NC, 2, 2, 2, 64, 512), BF),
            pltpu.VMEM((512, 896), BF),
            pltpu.VMEM((512, 896), BF),
            pltpu.VMEM((896, 512), BF),
            pltpu.VMEM((512, 896), BF),
            pltpu.VMEM((512, 896), BF),
            pltpu.VMEM((896, 512), BF),
            pltpu.VMEM((NC, 3, 2, 2, 2, 2) + blocks, BF),
            pltpu.VMEM((NC, 3, 2, 2, 2) + blocks, BF),
            pltpu.VMEM((NC, 3, 2, 2) + blocks, BF),
            pltpu.VMEM((NC, 3, 2) + blocks, BF),
            pltpu.VMEM((NC, 3) + blocks, BF),
            pltpu.VMEM((NC, 3, 2, 2, 2, 2) + blocks, BF),
            pltpu.VMEM((NC, 2, 128, 512), BF),
            pltpu.VMEM((NZ, 128, 512), BF),
            pltpu.VMEM((64, 512), BF),
            pltpu.VMEM((64, 512), BF),
            pltpu.VMEM((512, 896), BF),
            pltpu.VMEM((512, 896), BF),
            pltpu.VMEM((896, 512), BF),
            pltpu.VMEM((64, 512), BF),
            dma((3,)),
            dma((2,)),
            dma((2,)),
            dma((2, 4, 2)),
            dma((2, 4, 2)),
            dma((NC, 3, 8)),
            dma((NC, 3, 8)),
            dma((NZ,)),
            dma((NZ,)),
            dma((2,)),
            dma((4,)),
        ],
        compiler_params=pltpu.CompilerParams(
            collective_id=0, has_side_effects=True, vmem_limit_bytes=56 * 1024 * 1024
        ),
    )(tokens, grad_out, gate_codes, gate_scale, up_codes, up_scale, down_codes, down_scale)


def solution(mesh):
    in_specs = (
        P("hid", "wid"),
        P("hid", "wid"),
        P("wid", "hid"),
        P("wid", "hid"),
        P("wid", "hid"),
        P("wid", "hid"),
        P("hid", "wid"),
        P("hid", "wid"),
    )
    out_specs = (
        P("hid", "wid"),
        P("wid", "hid"),
        P("wid", "hid"),
        P("hid", "wid"),
        P(None, "wid", "hid"),
    )
    return jax.shard_map(body, mesh=mesh, in_specs=in_specs, out_specs=out_specs, check_vma=False)
```

time: 699 us -> 105 us (0.15)
  waiting for transfers between devices: 627 us -> 0 us
  Pallas kernels: 0 us -> 95.8 us
  matrix products: 26.9 us -> 0 us
  local copies, waits for them, and re-layouts: 22.2 us -> 8.11 us
  between operations: 14 us -> 0.64 us
    reduce_scatter x4 -> x0, waiting for transfers between devices: 385 us -> none  [the longest x1 191 us: body(): lax.psum_scatter(local_term.astype(jnp.bfloat16), 'hid', scatter_dimensio...]
    all_gather x5 -> x0, waiting for transfers between devices: 239 us -> none  [the longest x1 79 us: body(): lax.all_gather(tokens, 'hid', axis=0, tiled=True)]
    pallas_call x0 -> x1, Pallas kernels: none -> 95.8 us  [body(): pl.pallas_call(kernel, out_shape=(jax.ShapeDtypeStruct((64, 512), BF), ja...]
    dot_general x8 -> x0, matrix products: 26.9 us -> none  [the longest x3 12.6 us: contract_rows(): lax.dot_general(left, right, (((0,), (0,)), ((), ())), preferred_element_...]
    unnamed x34 -> x12, local copies, waits for them, and re-layouts: 15.2 us -> 8.11 us
  transfers between devices with their start and end apart: 9 -> 0, of which waited for: 9 -> 0; matrix products, arithmetic and copies ran while one was open for 7% -> 0% of each run, Pallas kernels for 0% -> 0%
where the time goes in v1:
time: 105 us
  Pallas kernels  95.8 us (91%)
  local copies, waits for them, and re-layouts  8.11 us (8%)
    pallas_call x1, Pallas kernels, body(): pl.pallas_call(kernel, out_shape=(jax.ShapeDtypeStruct((64, 512), BF), ja...  95.8 us
    unnamed x12, local copies, waits for them, and re-layouts  8.11 us

profile of v1, /device:TPU:1, one launch (start us, length us, event | category | flops | bytes accessed | tf_op | source)
XLA Modules:
  0.0 104.5 jit_solution(1711414392058304895)
XLA Ops:
  0.6 1.4 %copy.13.ds = f32[7,4]{1,0:T(8,128)} copy(f32[7,4]{0,1:T(4,128)} %param.15) | data formatting | bytes 224 | tf_op args[7]
  2.0 95.8 %shard_map.119 = (bf16[64,512]{1,0:T(8,128)(2,1)}, bf16[512,896]{1,0:T(8,128)(2,1)}, bf16[512,896]{1,0:T(8,128)(2,1)}, bf16[896,512]{1,0:T(8,128)(2,1)}, f32[3,4,7]{2,1,0:T(4,128)}) custom-call(bf16[64,512]{1,0:T(8,128)(2,1)} %tok_in.1, bf16[64,512]{1,0:T(8,128)(2,1)} %gro_in.1, bf16[512,896]{1,0:T(8,128)(2,1)} %gc_in.1, f32[4,7]{1,0:T(4,128)} %gs.1, ...), custom_call_target="tpu_custom_call" | custom-call | tf_op jit(solution)/shard_map/pallas_call | solution.py:303
  97.8 1.5 %copy.19 = bf16[64,512]{1,0:T(8,128)(2,1)} copy(bf16[64,512]{1,0:T(8,128)(2,1)} %get-tuple-element.10) | data formatting | bytes 131072
  99.2 0.0 copy-start.1
  99.2 2.3 %copy.20 = bf16[512,896]{1,0:T(8,128)(2,1)} copy(bf16[512,896]{1,0:T(8,128)(2,1)} %get-tuple-element.11) | data formatting | bytes 1835008
  101.5 0.0 copy-done.1
  101.5 0.0 copy-start
  101.5 0.9 copy.21
  102.4 0.6 copy-done
  103.0 0.0 copy-start.2
  103.0 0.9 copy.22
  103.9 0.0 copy-done.2
  103.9 0.6 copy.23
Async XLA Ops:
  99.2 2.3 %copy-start.1 = (bf16[512,896]{1,0:T(8,128)(2,1)S(1)}, bf16[512,896]{1,0:T(8,128)(2,1)}, u32[]{:S(2)}) copy-start(bf16[512,896]{1,0:T(8,128)(2,1)} %get-tuple-element.12) | copy-start | bytes 2752516
  101.5 1.5 %copy-start = (bf16[896,512]{1,0:T(8,128)(2,1)S(1)}, bf16[896,512]{1,0:T(8,128)(2,1)}, u32[]{:S(2)}) copy-start(bf16[896,512]{1,0:T(8,128)(2,1)} %get-tuple-element.13) | copy-start | bytes 2752516
  103.0 0.9 copy-start.2

commit v2 on v1

v2 whole, which is shorter than its diff:
```python
import jax
import jax.numpy as jnp
from jax import lax
from jax.experimental import pallas as pl
from jax.experimental.pallas import tpu as pltpu
from jax.sharding import PartitionSpec as P

BLK = 128
NZ = 8
CHUNKS = (((5, 0), (6, 1), (2, 1), (7, 1)), ((1, 1), (7, 0), (2, 0), (6, 0)), ((0, 0), (4, 1), (3, 1), (4, 0)), ((3, 0), (0, 1), (1, 0), (5, 1)))
CHAIN = ((2, 0), (2, 1), (4, 0), (4, 1))
STEPS = (
    ("Dq", 0), ("Dq", 1), ("Dq", 2), ("F", 1, 0, 0), ("Fx", 0), ("F", 1, 0, 1),
    ("Fx", 1), ("F", 2, 0, 0), ("F", 1, 1, 0), ("S", 1, 1), ("S", 1, 0), ("F", 2, 0, 1),
    ("C", 1, 1), ("C", 1, 0), ("F", 1, 1, 1), ("S", 1, 2), ("F", 3, 0, 0), ("C", 1, 2),
    ("F", 2, 1, 0), ("S", 0, 1), ("S", 0, 0), ("P1", 1, 1), ("P1", 1, 0), ("F", 3, 0, 1),
    ("C", 0, 1), ("C", 0, 0), ("F", 2, 1, 1), ("S", 0, 2), ("P1", 1, 2), ("F", 4, 0, 0),
    ("P2", 1, 0), ("C", 0, 2), ("P2", 1, 1), ("F", 3, 1, 0), ("F", 4, 0, 1), ("S", 3, 1),
    ("S", 3, 0), ("P1", 0, 0), ("P1", 0, 1), ("F", 3, 1, 1), ("S", 3, 2), ("C", 3, 1),
    ("C", 3, 0), ("P2", 1, 2), ("C", 3, 2), ("F", 4, 1, 0), ("S", 2, 0), ("S", 2, 1),
    ("P1", 0, 2), ("P2", 0, 0), ("F", 4, 1, 1), ("S", 2, 2), ("C", 2, 0), ("P2", 0, 1),
    ("C", 2, 1), ("C", 2, 2), ("P1", 3, 0), ("P1", 3, 1), ("N", 1), ("P1", 3, 2),
    ("P2", 0, 2), ("P1", 2, 1), ("P1", 2, 0), ("P1", 2, 2), ("P2", 3, 0), ("A3", 1, 1),
    ("A3", 1, 2), ("P2", 3, 1), ("N", 0), ("A3", 1, 0), ("P2", 3, 2), ("P2", 2, 0),
    ("P2", 2, 1), ("P2", 2, 2), ("A2", 1, 2), ("A3", 0, 2), ("A2", 1, 1), ("A3", 0, 0),
    ("A3", 0, 1), ("A2", 1, 0), ("N", 3), ("N", 2), ("A2", 0, 2), ("A1", 1, 2),
    ("A1", 1, 1), ("A2", 0, 1), ("A1", 1, 0), ("G", 1, 2), ("A3", 3, 0), ("T", 1),
    ("Z", 1, 2, 0), ("Z", 1, 6, 0), ("A3", 2, 1), ("A3", 2, 0), ("A3", 2, 2), ("A3", 3, 1),
    ("A3", 3, 2), ("A2", 0, 0), ("G", 1, 0), ("G", 1, 1), ("A1", 0, 2), ("A1", 0, 1),
    ("A2", 2, 1), ("Z", 1, 7, 0), ("A2", 2, 2), ("G", 0, 2), ("T", 0), ("Z", 0, 5, 0),
    ("Z", 0, 6, 1), ("Z", 0, 2, 1), ("A2", 3, 1), ("A2", 2, 0), ("A2", 3, 0), ("A2", 3, 2),
    ("G", 0, 1), ("A1", 0, 0), ("A1", 2, 1), ("A1", 2, 2), ("Z", 1, 1, 1), ("G", 0, 0),
    ("G", 2, 1), ("T", 2), ("Z", 2, 4, 1), ("Z", 2, 3, 1), ("Z", 2, 4, 0), ("A1", 2, 0),
    ("A1", 3, 2), ("A1", 3, 1), ("G", 2, 2), ("G", 2, 0), ("Z", 0, 7, 1), ("A1", 3, 0),
    ("T", 3), ("Z", 3, 1, 0), ("Z", 3, 5, 1), ("G", 3, 0), ("G", 3, 1), ("G", 3, 2),
    ("Z", 3, 3, 0), ("X",), ("E",),
)
POS = {block: (c, i) for c, blocks in enumerate(CHUNKS) for i, block in enumerate(blocks)}
NC = len(CHUNKS)
ROWS = 16
ORDER = ((0, 1, 2), (1, 2, 0), (2, 0, 1))
BF = jnp.bfloat16
F32 = jnp.float32


def matmul(left, right, dims=((1,), (0,))):
    return lax.dot_general(left, right, (dims, ((), ())), preferred_element_type=F32)


def far(block):
    return min(block[0], NZ - block[0])


def way_of(block):
    r, xh = block
    return 1 if r < 4 or (r == 4 and xh == 0) else -1


def chained(block):
    return (far(block), block[1]) in CHAIN


def feeder(block):
    r, xh = block
    before = ((r + way_of(block)) % NZ, xh)
    if r == 0 or r == 4 or not chained(before) or way_of(before) != way_of(block):
        return None
    return before


BLOCKS = [(r, xh) for r in range(1, NZ) for xh in range(2)]
HOME = [block for block in BLOCKS if far(block) == 1 or not chained(block)]
HOPS = sorted({1, NZ - 1} | {r for r, xh in BLOCKS if not chained((r, xh))})


def kernel(
    tok_in, gro_in, gc_in, gs, uc_in, us, dc_in, ds,
    gt_out, gg_out, gu_out, gd_out, bn_out,
    X, codes_g, codes_u, codes_d, wg, wu, wd, part, rb0, rb1, rb2, rb3, ag, term, zin, xsend, xrecv,
    acc_g, acc_u, acc_d,
    loc_sem, own_sem, xs_sem, ring_s, ring_r, wid_s, wid_r, z_s, z_r, xf_sem,
):
    hid, wid = lax.axis_index("hid"), lax.axis_index("wid")
    z, xhi = hid // 2, hid % 2
    y, xlo, core = wid // 4, (wid // 2) % 2, wid % 2
    bit_a, bit_b = (y + y // 2) % 2, y // 2
    bits = (xlo, bit_a, bit_b)
    core_peer = wid + 1 - 2 * core
    x_peer = (y * 2 + 1 - xlo) * 2 + core
    a_peer = ((y + 1 - 2 * (y % 2)) * 2 + xlo) * 2 + core
    b_peer = ((3 - y) * 2 + xlo) * 2 + core
    pair_peer = (x_peer, a_peer, b_peer)
    xhi_peer = z * 2 + 1 - xhi

    def z_peer(r):
        return ((z + r) % NZ) * 2 + xhi

    barrier = pltpu.get_barrier_semaphore()
    for peer in (core_peer,) + pair_peer:
        pl.semaphore_signal(barrier, inc=1, device_id={"wid": peer}, device_id_type=pl.DeviceIdType.MESH)
    for peer in [xhi_peer] + [z_peer(r) for r in sorted(set(HOPS) | {NZ - r for r in HOPS})]:
        pl.semaphore_signal(barrier, inc=1, device_id={"hid": peer}, device_id_type=pl.DeviceIdType.MESH)

    def rows(block, g):
        c, i = POS[block]
        return X.at[c, g, i]

    own = [
        pltpu.make_async_copy(tok_in, rows((0, 0), 0), own_sem.at[0]),
        pltpu.make_async_copy(gro_in, rows((0, 0), 1), own_sem.at[1]),
    ]
    loads = [
        pltpu.make_async_copy(gc_in, codes_g, loc_sem.at[0]),
        pltpu.make_async_copy(uc_in, codes_u, loc_sem.at[1]),
        pltpu.make_async_copy(dc_in, codes_d, loc_sem.at[2]),
    ]
    for copy in own + loads:
        copy.start()
    for copy in own:
        copy.wait()
    pl.semaphore_wait(barrier, 5 + len(set(HOPS) | {NZ - r for r in HOPS}))

    sends = []

    def remote(src, dst, send, recv, where):
        return pltpu.make_async_remote_copy(
            src_ref=src, dst_ref=dst, send_sem=send, recv_sem=recv,
            device_id=where, device_id_type=pl.DeviceIdType.MESH,
        )

    def go(copy):
        copy.start()
        sends.append(copy)

    x_copy = [
        remote(rows((0, 0), g), rows((0, 1), g), xs_sem.at[0, g], xs_sem.at[1, g], {"hid": xhi_peer}) for g in range(2)
    ]
    ring = {}
    for way, sign in ((0, -1), (1, 1)):
        for j in range(1, 5):
            for xh in range(2):
                for g in range(2):
                    if j < 4 or g == way:
                        ring[way, j, xh, g] = remote(
                            rows(((sign * (j - 1)) % NZ, xh), g), rows(((sign * j) % NZ, xh), g),
                            ring_s.at[way, j - 1, xh, g], ring_r.at[way, j - 1, xh, g], {"hid": z_peer(-sign)},
                        )

    def forward(j, xh, g):
        for way in range(2):
            if (way, j, xh, g) in ring:
                ring[way, j, xh, g].wait_recv()
                if (way, j + 1, xh, g) in ring:
                    go(ring[way, j + 1, xh, g])

    def forward_x(g):
        x_copy[g].wait_recv()
        for way in range(2):
            go(ring[way, 1, 1, g])

    def dequant(load, codes, scales, weight):
        load.wait()
        height, cols = weight.shape
        for i in range(height // BLK):
            for j in range(cols // BLK):
                at = (slice(i * BLK, (i + 1) * BLK), slice(j * BLK, (j + 1) * BLK))
                weight[at] = (codes[at].astype(F32) * scales(i, j)).astype(BF)

    for g in range(2):
        go(x_copy[g])
    for g in range(2):
        for way in range(2):
            go(ring[way, 1, 0, g])

    def at_bits(free, other=None):
        index = []
        for d in range(3):
            if d in free:
                index.append(slice(None))
            elif d == other:
                index.append(1 - bits[d])
            else:
                index.append(bits[d])
        return tuple(index)

    def core_sum(c, k):
        return remote(part.at[c, k, 1 - core], rb0.at[c, k], wid_s.at[c, k, 0], wid_r.at[c, k, 0], {"wid": core_peer})

    def pair_sum(c, k, s):
        order = ORDER[k]
        index = at_bits(order[s:], order[s - 1])
        return remote(
            part.at[(c, k, core) + index], (rb1, rb2, rb3)[s - 1].at[c, k],
            wid_s.at[c, k, s], wid_r.at[c, k, s], {"wid": pair_peer[order[s - 1]]},
        )

    def pair_gather(c, k, s):
        order = ORDER[k]
        ref = ag.at[(c, k, core) + at_bits(order[s:])]
        return remote(ref, ref, wid_s.at[c, k, 7 - s], wid_r.at[c, k, 7 - s], {"wid": pair_peer[order[s - 1]]})

    def core_gather(c, k):
        ref = ag.at[c, k, core]
        return remote(ref, ref, wid_s.at[c, k, 7], wid_r.at[c, k, 7], {"wid": core_peer})

    def add_into(ref, other):
        ref[...] = (ref[...].astype(F32) + other[...].astype(F32)).astype(BF)

    def step_partial(c, k):
        left = X[c, k // 2].reshape(256, 512)
        whole = matmul(left, wd[...], ((1,), (1,))) if k == 2 else matmul(left, (wg, wu)[k][...])
        part[c, k] = whole.astype(BF).reshape(2, 2, 2, 2, ROWS, 896)
        go(core_sum(c, k))

    def step_core(c, k):
        core_sum(c, k).wait_recv()
        add_into(part.at[c, k, core], rb0.at[c, k])
        go(pair_sum(c, k, 1))

    def step_pair(c, k, s):
        pair_sum(c, k, s).wait_recv()
        add_into(part.at[(c, k, core) + at_bits(ORDER[k][s:])], (rb1, rb2)[s - 1].at[c, k])
        go(pair_sum(c, k, s + 1))

    def step_nonlinear(c):
        sums = []
        for k in range(3):
            pair_sum(c, k, 3).wait_recv()
            sums.append(part[(c, k, core) + bits].astype(F32) + rb3[c, k].astype(F32))
        gate, upper, grad = sums
        sigma = jax.nn.sigmoid(gate)
        active = gate * sigma
        ag[(c, 1, core) + bits] = (grad * upper * sigma * (1.0 + gate * (1.0 - sigma))).astype(BF)
        go(pair_gather(c, 1, 3))
        ag[(c, 2, core) + bits] = (grad * active).astype(BF)
        go(pair_gather(c, 2, 3))
        ag[(c, 0, core) + bits] = (active * upper).astype(BF)
        go(pair_gather(c, 0, 3))

    def step_gather(c, k, s):
        pair_gather(c, k, s).wait_recv()
        go(pair_gather(c, k, s - 1) if s > 1 else core_gather(c, k))

    def z_send(block):
        r, xh = block
        c, i = POS[block]
        hop = way_of(block) % NZ if chained(block) else r
        return remote(term.at[c, i], zin.at[r, xh], z_s.at[r, xh], z_r.at[r, xh], {"hid": z_peer(hop)})

    landed = set()

    def landing(c, k):
        if (c, k) not in landed:
            landed.add((c, k))
            core_gather(c, k).wait_recv()
        return ag[c, k].reshape(256, 896)

    def step_term(c):
        total = matmul(landing(c, 1), wg[...], ((1,), (1,)))
        total += matmul(landing(c, 2), wu[...], ((1,), (1,)))
        term[c] = total.astype(BF).reshape(4, 64, 512)

    def step_home(c, r, xh):
        c, i = POS[r, xh]
        before = feeder((r, xh))
        if before is not None:
            z_send(before).wait_recv()
            add_into(term.at[c, i], zin.at[before])
        go(z_send((r, xh)))

    def home_sum(xh):
        total = term[POS[0, xh]].astype(F32)
        for block in HOME:
            if block[1] == xh:
                z_send(block).wait_recv()
                total += zin[block].astype(F32)
        return total

    last = remote(xsend, xrecv, xf_sem.at[0], xf_sem.at[1], {"hid": xhi_peer})

    def step_cross():
        xsend[...] = home_sum(1).astype(BF)
        go(last)

    def step_last():
        total = home_sum(0)
        last.wait_recv()
        gt_out[...] = (total + xrecv[...].astype(F32)).astype(BF)

    def block_sums(full):
        height, cols = full.shape
        sums = jnp.sum((full * full).reshape(height // BLK, BLK, cols), axis=1)
        of_block = (
            lax.broadcasted_iota(jnp.int32, (cols // BLK, cols), 1) // BLK
            == lax.broadcasted_iota(jnp.int32, (cols // BLK, cols), 0)
        ).astype(F32)
        return sums, of_block

    def exact(left, right):
        return lax.dot_general(
            left, right, (((1,), (1,)), ((), ())), precision=lax.Precision.HIGHEST, preferred_element_type=F32
        )

    seen = {0: 0, 1: 0, 2: 0}

    def step_grad(c, k):
        d = landing(c, k)
        if k == 0:
            full = matmul(d, X[c, 1].reshape(256, 512), ((0,), (0,)))
        else:
            full = matmul(X[c, 0].reshape(256, 512), d, ((0,), (0,)))
        acc = (acc_d, acc_g, acc_u)[k]
        if seen[k]:
            full += acc[...]
        seen[k] += 1
        if seen[k] < NC:
            acc[...] = full
            return
        out, row = ((gd_out, 2), (gg_out, 0), (gu_out, 1))[k]
        out[...] = full.astype(BF)
        sums, of_block = block_sums(full)
        bn_out[row] = exact(of_block, sums) if k == 0 else exact(sums, of_block)

    do = {
        "Dq": lambda k: dequant(
            loads[k],
            (codes_g, codes_u, codes_d)[k],
            (lambda i, j: gs[i, j], lambda i, j: us[i, j], lambda i, j: ds[j, i])[k],
            (wg, wu, wd)[k],
        ),
        "Fx": forward_x,
        "F": forward,
        "S": step_partial,
        "C": step_core,
        "P1": lambda c, k: step_pair(c, k, 1),
        "P2": lambda c, k: step_pair(c, k, 2),
        "N": step_nonlinear,
        "A3": lambda c, k: step_gather(c, k, 3),
        "A2": lambda c, k: step_gather(c, k, 2),
        "A1": lambda c, k: step_gather(c, k, 1),
        "T": step_term,
        "Z": step_home,
        "G": step_grad,
        "X": step_cross,
        "E": step_last,
    }
    for name, *at in STEPS:
        do[name](*at)
    for copy in sends:
        copy.wait_send()


def body(tokens, grad_out, gate_codes, gate_scale, up_codes, up_scale, down_codes, down_scale):
    hbm = pl.BlockSpec(memory_space=pl.ANY)
    smem = pl.BlockSpec(memory_space=pltpu.SMEM)
    vmem = pl.BlockSpec(memory_space=pltpu.VMEM)
    dma = pltpu.SemaphoreType.DMA
    blocks = (ROWS, 896)
    shapes = (
        jax.ShapeDtypeStruct((64, 512), BF),
        jax.ShapeDtypeStruct((512, 896), BF),
        jax.ShapeDtypeStruct((512, 896), BF),
        jax.ShapeDtypeStruct((896, 512), BF),
        jax.ShapeDtypeStruct((3, 4, 7), F32),
    )
    found = pl.pallas_call(
        kernel,
        out_shape=tuple(pltpu.VMEM(shape.shape, shape.dtype) for shape in shapes),
        in_specs=[hbm, hbm, hbm, smem, hbm, smem, hbm, smem],
        out_specs=(vmem,) * 5,
        scratch_shapes=[
            pltpu.VMEM((NC, 2, 4, 64, 512), BF),
            pltpu.VMEM((512, 896), BF),
            pltpu.VMEM((512, 896), BF),
            pltpu.VMEM((896, 512), BF),
            pltpu.VMEM((512, 896), BF),
            pltpu.VMEM((512, 896), BF),
            pltpu.VMEM((896, 512), BF),
            pltpu.VMEM((NC, 3, 2, 2, 2, 2) + blocks, BF),
            pltpu.VMEM((NC, 3, 2, 2, 2) + blocks, BF),
            pltpu.VMEM((NC, 3, 2, 2) + blocks, BF),
            pltpu.VMEM((NC, 3, 2) + blocks, BF),
            pltpu.VMEM((NC, 3) + blocks, BF),
            pltpu.VMEM((NC, 3, 2, 2, 2, 2) + blocks, BF),
            pltpu.VMEM((NC, 4, 64, 512), BF),
            pltpu.VMEM((NZ, 2, 64, 512), BF),
            pltpu.VMEM((64, 512), BF),
            pltpu.VMEM((64, 512), BF),
            pltpu.VMEM((512, 896), F32),
            pltpu.VMEM((512, 896), F32),
            pltpu.VMEM((896, 512), F32),
            dma((3,)),
            dma((2,)),
            dma((2, 2)),
            dma((2, 4, 2, 2)),
            dma((2, 4, 2, 2)),
            dma((NC, 3, 8)),
            dma((NC, 3, 8)),
            dma((NZ, 2)),
            dma((NZ, 2)),
            dma((2,)),
        ],
        compiler_params=pltpu.CompilerParams(
            collective_id=0, has_side_effects=True, vmem_limit_bytes=60 * 1024 * 1024
        ),
    )(tokens, grad_out, gate_codes, gate_scale, up_codes, up_scale, down_codes, down_scale.T)
    return found


def solution(mesh):
    in_specs = (
        P("hid", "wid"),
        P("hid", "wid"),
        P("wid", "hid"),
        P("wid", "hid"),
        P("wid", "hid"),
        P("wid", "hid"),
        P("hid", "wid"),
        P("hid", "wid"),
    )
    out_specs = (
        P("hid", "wid"),
        P("wid", "hid"),
        P("wid", "hid"),
        P("hid", "wid"),
        P(None, "wid", "hid"),
    )
    return jax.shard_map(body, mesh=mesh, in_specs=in_specs, out_specs=out_specs, check_vma=False)
```

time: 105 us -> 89.6 us (0.85)
  Pallas kernels: 95.8 us -> 83.8 us
  local copies, waits for them, and re-layouts: 8.11 us -> 3.99 us
    pallas_call x1, Pallas kernels: 95.8 us -> 83.8 us  [body(): pl.pallas_call(kernel, out_shape=tuple((pltpu.VMEM(shape.shape, shape.dty...]
    unnamed x12 -> x5, local copies, waits for them, and re-layouts: 8.11 us -> 3.99 us
where the time goes in v2:
time: 89.6 us; the launch traced here: 88.5 us
  Pallas kernels  83.8 us (94%)
  local copies, waits for them, and re-layouts  3.99 us (4%)
    pallas_call x1, Pallas kernels, body(): pl.pallas_call(kernel, out_shape=tuple((pltpu.VMEM(shape.shape, shape.dty...  83.8 us
    unnamed x5, local copies, waits for them, and re-layouts  3.99 us

profile of v2, /device:TPU:1, one launch (start us, length us, event | category | flops | bytes accessed | tf_op | source)
XLA Modules:
  0.0 88.5 jit_solution(885413298387431778)
XLA Ops:
  0.6 83.8 %shard_map.119 = (bf16[64,512]{1,0:T(8,128)(2,1)S(1)}, bf16[512,896]{1,0:T(8,128)(2,1)S(1)}, bf16[512,896]{1,0:T(8,128)(2,1)S(1)}, bf16[896,512]{1,0:T(8,128)(2,1)S(1)}, f32[3,4,7]{2,1,0:T(4,128)S(1)}) custom-call(bf16[64,512]{1,0:T(8,128)(2,1)} %tok_in.1, bf16[64,512]{1,0:T(8,128)(2,1)} %gro_in.1, bf16[512,896]{1,0:T(8,128)(2,1)} %gc_in.1, f32[4,7]{1,0:T(4,128)} %gs.1, ...), custom_call_target="tpu_custom_call" | custom-call | tf_op jit(solution)/shard_map/pallas_call | solution.py:366
  84.5 0.6 copy.18
  85.1 0.6 copy.22
  85.7 0.9 %copy.19 = bf16[512,896]{1,0:T(8,128)(2,1)} copy(bf16[512,896]{1,0:T(8,128)(2,1)S(1)} %get-tuple-element.6) | data formatting | bytes 1835008
  86.6 0.9 %copy.20 = bf16[512,896]{1,0:T(8,128)(2,1)} copy(bf16[512,896]{1,0:T(8,128)(2,1)S(1)} %get-tuple-element.7) | data formatting | bytes 1835008
  87.6 0.9 %copy.21 = bf16[896,512]{1,0:T(8,128)(2,1)} copy(bf16[896,512]{1,0:T(8,128)(2,1)S(1)} %get-tuple-element.8) | data formatting | bytes 1835008

commit v3 on v2

--- a/solution.py
+++ b/solution.py
@@ -7,33 +7,35 @@
 
 BLK = 128
 NZ = 8
-CHUNKS = (((5, 0), (6, 1), (2, 1), (7, 1)), ((1, 1), (7, 0), (2, 0), (6, 0)), ((0, 0), (4, 1), (3, 1), (4, 0)), ((3, 0), (0, 1), (1, 0), (5, 1)))
-CHAIN = ((2, 0), (2, 1), (4, 0), (4, 1))
+CHUNKS = (((2, 0), (7, 0), (0, 1), (6, 0)), ((1, 1), (1, 0), (0, 0), (5, 0)), ((3, 1), (7, 1), (5, 1), (4, 1)), ((2, 1), (6, 1), (4, 0), (3, 0)))
+CHAIN = ((2, 0), (2, 1), (3, 1), (4, 0), (4, 1))
+DIRECT = ((1, 1), (2, 1), (5, 1), (7, 1))
+ACROSS = (1,)
+SPREAD = (2,)
 STEPS = (
     ("Dq", 0), ("Dq", 1), ("Dq", 2), ("F", 1, 0, 0), ("Fx", 0), ("F", 1, 0, 1),
-    ("Fx", 1), ("F", 2, 0, 0), ("F", 1, 1, 0), ("S", 1, 1), ("S", 1, 0), ("F", 2, 0, 1),
-    ("C", 1, 1), ("C", 1, 0), ("F", 1, 1, 1), ("S", 1, 2), ("F", 3, 0, 0), ("C", 1, 2),
-    ("F", 2, 1, 0), ("S", 0, 1), ("S", 0, 0), ("P1", 1, 1), ("P1", 1, 0), ("F", 3, 0, 1),
-    ("C", 0, 1), ("C", 0, 0), ("F", 2, 1, 1), ("S", 0, 2), ("P1", 1, 2), ("F", 4, 0, 0),
-    ("P2", 1, 0), ("C", 0, 2), ("P2", 1, 1), ("F", 3, 1, 0), ("F", 4, 0, 1), ("S", 3, 1),
-    ("S", 3, 0), ("P1", 0, 0), ("P1", 0, 1), ("F", 3, 1, 1), ("S", 3, 2), ("C", 3, 1),
-    ("C", 3, 0), ("P2", 1, 2), ("C", 3, 2), ("F", 4, 1, 0), ("S", 2, 0), ("S", 2, 1),
-    ("P1", 0, 2), ("P2", 0, 0), ("F", 4, 1, 1), ("S", 2, 2), ("C", 2, 0), ("P2", 0, 1),
-    ("C", 2, 1), ("C", 2, 2), ("P1", 3, 0), ("P1", 3, 1), ("N", 1), ("P1", 3, 2),
-    ("P2", 0, 2), ("P1", 2, 1), ("P1", 2, 0), ("P1", 2, 2), ("P2", 3, 0), ("A3", 1, 1),
-    ("A3", 1, 2), ("P2", 3, 1), ("N", 0), ("A3", 1, 0), ("P2", 3, 2), ("P2", 2, 0),
-    ("P2", 2, 1), ("P2", 2, 2), ("A2", 1, 2), ("A3", 0, 2), ("A2", 1, 1), ("A3", 0, 0),
-    ("A3", 0, 1), ("A2", 1, 0), ("N", 3), ("N", 2), ("A2", 0, 2), ("A1", 1, 2),
-    ("A1", 1, 1), ("A2", 0, 1), ("A1", 1, 0), ("G", 1, 2), ("A3", 3, 0), ("T", 1),
-    ("Z", 1, 2, 0), ("Z", 1, 6, 0), ("A3", 2, 1), ("A3", 2, 0), ("A3", 2, 2), ("A3", 3, 1),
-    ("A3", 3, 2), ("A2", 0, 0), ("G", 1, 0), ("G", 1, 1), ("A1", 0, 2), ("A1", 0, 1),
-    ("A2", 2, 1), ("Z", 1, 7, 0), ("A2", 2, 2), ("G", 0, 2), ("T", 0), ("Z", 0, 5, 0),
-    ("Z", 0, 6, 1), ("Z", 0, 2, 1), ("A2", 3, 1), ("A2", 2, 0), ("A2", 3, 0), ("A2", 3, 2),
-    ("G", 0, 1), ("A1", 0, 0), ("A1", 2, 1), ("A1", 2, 2), ("Z", 1, 1, 1), ("G", 0, 0),
-    ("G", 2, 1), ("T", 2), ("Z", 2, 4, 1), ("Z", 2, 3, 1), ("Z", 2, 4, 0), ("A1", 2, 0),
-    ("A1", 3, 2), ("A1", 3, 1), ("G", 2, 2), ("G", 2, 0), ("Z", 0, 7, 1), ("A1", 3, 0),
-    ("T", 3), ("Z", 3, 1, 0), ("Z", 3, 5, 1), ("G", 3, 0), ("G", 3, 1), ("G", 3, 2),
-    ("Z", 3, 3, 0), ("X",), ("E",),
+    ("Fx", 1), ("F", 2, 0, 0), ("S", 0, 1), ("S", 0, 0), ("F", 2, 0, 1), ("S", 0, 2),
+    ("F", 1, 1, 0), ("C", 0, 1), ("C", 0, 0), ("C", 0, 2), ("F", 3, 0, 0), ("S", 1, 1),
+    ("S", 1, 0), ("F", 1, 1, 1), ("F", 3, 0, 1), ("S", 1, 2), ("C", 1, 1), ("C", 1, 0),
+    ("F", 2, 1, 0), ("P1", 0, 1), ("C", 1, 2), ("P1", 0, 0), ("F", 4, 0, 0), ("S", 3, 1),
+    ("S", 3, 0), ("P1", 0, 2), ("F", 2, 1, 1), ("C", 3, 1), ("F", 4, 0, 1), ("S", 3, 2),
+    ("C", 3, 0), ("P2", 0, 1), ("P1", 1, 0), ("P1", 1, 1), ("F", 3, 1, 0), ("P2", 0, 0),
+    ("C", 3, 2), ("P2", 0, 2), ("P1", 1, 2), ("F", 3, 1, 1), ("P2", 1, 1), ("P1", 3, 1),
+    ("F", 4, 1, 0), ("S", 2, 1), ("S", 2, 0), ("P1", 3, 0), ("P2", 1, 0), ("N", 0),
+    ("F", 4, 1, 1), ("P2", 1, 2), ("S", 2, 2), ("C", 2, 0), ("C", 2, 1), ("P1", 3, 2),
+    ("P2", 3, 1), ("C", 2, 2), ("P2", 3, 0), ("A3", 0, 1), ("A3", 0, 2), ("A3", 0, 0),
+    ("N", 1), ("P1", 2, 0), ("P1", 2, 1), ("P2", 3, 2), ("P1", 2, 2), ("A2", 0, 0),
+    ("A3", 1, 2), ("A2", 0, 2), ("A2", 0, 1), ("A3", 1, 1), ("A3", 1, 0), ("N", 3),
+    ("N", 2), ("A1", 0, 1), ("A1", 0, 0), ("A1", 0, 2), ("A2", 1, 0), ("G", 0, 1),
+    ("A2", 1, 1), ("A2", 1, 2), ("A3", 3, 2), ("G", 0, 0), ("A3", 3, 1), ("A3", 3, 0),
+    ("T", 0), ("Z", 0, 2, 0), ("Z", 0, 6, 0), ("X",), ("G", 0, 2), ("A2", 2, 0),
+    ("A2", 2, 2), ("A2", 2, 1), ("A1", 1, 1), ("Z", 0, 7, 0), ("A1", 1, 0), ("A1", 1, 2),
+    ("A2", 3, 0), ("G", 1, 1), ("A2", 3, 1), ("A2", 3, 2), ("G", 1, 0), ("T", 1),
+    ("Z", 1, 1, 1), ("Z", 1, 1, 0), ("Z", 1, 5, 0), ("A1", 2, 1), ("G", 1, 2), ("A1", 2, 2),
+    ("G", 2, 1), ("A1", 2, 0), ("T", 2), ("Z", 2, 3, 1), ("Z", 2, 4, 1), ("A1", 3, 1),
+    ("A1", 3, 2), ("G", 2, 2), ("G", 2, 0), ("A1", 3, 0), ("T", 3), ("Z", 3, 6, 1),
+    ("Z", 3, 4, 0), ("G", 3, 0), ("Z", 3, 2, 1), ("G", 3, 1), ("G", 3, 2), ("Z", 2, 5, 1),
+    ("Z", 2, 7, 1), ("Z", 3, 3, 0), ("E",),
 )
 POS = {block: (c, i) for c, blocks in enumerate(CHUNKS) for i, block in enumerate(blocks)}
 NC = len(CHUNKS)
@@ -57,7 +59,7 @@
 
 
 def chained(block):
-    return (far(block), block[1]) in CHAIN
+    return (far(block), block[1]) in CHAIN and block not in DIRECT
 
 
 def feeder(block):
@@ -70,7 +72,9 @@
 
 BLOCKS = [(r, xh) for r in range(1, NZ) for xh in range(2)]
 HOME = [block for block in BLOCKS if far(block) == 1 or not chained(block)]
-HOPS = sorted({1, NZ - 1} | {r for r, xh in BLOCKS if not chained((r, xh))})
+HOPS = {1, NZ - 1} | {r for r, xh in BLOCKS if not chained((r, xh)) and (r, xh) not in DIRECT}
+HOPS = sorted(HOPS | {NZ - r for r in HOPS})
+SIDE = sorted({r for r, _ in DIRECT} | {NZ - r for r, _ in DIRECT})
 
 
 def kernel(
@@ -78,7 +82,7 @@
     gt_out, gg_out, gu_out, gd_out, bn_out,
     X, codes_g, codes_u, codes_d, wg, wu, wd, part, rb0, rb1, rb2, rb3, ag, term, zin, xsend, xrecv,
     acc_g, acc_u, acc_d,
-    loc_sem, own_sem, xs_sem, ring_s, ring_r, wid_s, wid_r, z_s, z_r, xf_sem,
+    loc_sem, own_sem, xs_sem, ring_s, ring_r, side_s, side_r, wid_s, wid_r, z_s, z_r, xf_sem,
 ):
     hid, wid = lax.axis_index("hid"), lax.axis_index("wid")
     z, xhi = hid // 2, hid % 2
@@ -86,19 +90,28 @@
     bit_a, bit_b = (y + y // 2) % 2, y // 2
     bits = (xlo, bit_a, bit_b)
     core_peer = wid + 1 - 2 * core
-    x_peer = (y * 2 + 1 - xlo) * 2 + core
-    a_peer = ((y + 1 - 2 * (y % 2)) * 2 + xlo) * 2 + core
-    b_peer = ((3 - y) * 2 + xlo) * 2 + core
-    pair_peer = (x_peer, a_peer, b_peer)
+
+    def flipped(dims):
+        row = (y, y + 1 - 2 * (y % 2), 3 - y, (y + 2) % 4)[(1 in dims) + 2 * (2 in dims)]
+        return (row * 2 + (1 - xlo if 0 in dims else xlo)) * 2 + core
+
+    pair_peer = tuple(flipped((d,)) for d in range(3))
     xhi_peer = z * 2 + 1 - xhi
 
     def z_peer(r):
         return ((z + r) % NZ) * 2 + xhi
 
+    def side_peer(r):
+        return ((z + r) % NZ) * 2 + 1 - xhi
+
     barrier = pltpu.get_barrier_semaphore()
-    for peer in (core_peer,) + pair_peer:
+    near = (core_peer,) + pair_peer
+    if SPREAD:
+        near += tuple(flipped(order[1:]) for order in ORDER)
+    across = [xhi_peer] + [z_peer(r) for r in HOPS] + [side_peer(r) for r in SIDE]
+    for peer in near:
         pl.semaphore_signal(barrier, inc=1, device_id={"wid": peer}, device_id_type=pl.DeviceIdType.MESH)
-    for peer in [xhi_peer] + [z_peer(r) for r in sorted(set(HOPS) | {NZ - r for r in HOPS})]:
+    for peer in across:
         pl.semaphore_signal(barrier, inc=1, device_id={"hid": peer}, device_id_type=pl.DeviceIdType.MESH)
 
     def rows(block, g):
@@ -118,7 +131,7 @@
         copy.start()
     for copy in own:
         copy.wait()
-    pl.semaphore_wait(barrier, 5 + len(set(HOPS) | {NZ - r for r in HOPS}))
+    pl.semaphore_wait(barrier, len(near) + len(across))
 
     sends = []
 
@@ -140,23 +153,39 @@
         for j in range(1, 5):
             for xh in range(2):
                 for g in range(2):
-                    if j < 4 or g == way:
+                    if (j < 4 or g == way) and not (xh == 1 and j in ACROSS):
                         ring[way, j, xh, g] = remote(
                             rows(((sign * (j - 1)) % NZ, xh), g), rows(((sign * j) % NZ, xh), g),
                             ring_s.at[way, j - 1, xh, g], ring_r.at[way, j - 1, xh, g], {"hid": z_peer(-sign)},
                         )
 
+    side = {}
+    for way, sign in ((0, -1), (1, 1)):
+        for j in ACROSS:
+            for g in range(2):
+                if j < 4 or g == way:
+                    side[way, j, g] = remote(
+                        rows(((sign * j) % NZ, 0), g), rows(((sign * j) % NZ, 1), g),
+                        side_s.at[way, j - 1, g], side_r.at[way, j - 1, g], {"hid": xhi_peer},
+                    )
+
     def forward(j, xh, g):
         for way in range(2):
-            if (way, j, xh, g) in ring:
-                ring[way, j, xh, g].wait_recv()
-                if (way, j + 1, xh, g) in ring:
-                    go(ring[way, j + 1, xh, g])
+            came = side.get((way, j, g)) if xh == 1 and j in ACROSS else ring.get((way, j, xh, g))
+            if came is not None:
+                came.wait_recv()
+        for way in range(2):
+            if (way, j + 1, xh, g) in ring:
+                go(ring[way, j + 1, xh, g])
+        for way in range(2):
+            if xh == 0 and (way, j, g) in side:
+                go(side[way, j, g])
 
     def forward_x(g):
         x_copy[g].wait_recv()
         for way in range(2):
-            go(ring[way, 1, 1, g])
+            if (way, 1, 1, g) in ring:
+                go(ring[way, 1, 1, g])
 
     def dequant(load, codes, scales, weight):
         load.wait()
@@ -203,6 +232,26 @@
         ref = ag.at[c, k, core]
         return remote(ref, ref, wid_s.at[c, k, 7], wid_r.at[c, k, 7], {"wid": core_peer})
 
+    def spread(k, i):
+        return ((ORDER[k][1],), (ORDER[k][2],), ORDER[k][1:])[i]
+
+    def spread_sum(c, k, i):
+        crossed = spread(k, i)
+        index = tuple(1 - bits[d] if d in crossed else bits[d] for d in range(3))
+        sem = (2, 3, 8)[i]
+        return remote(
+            part.at[(c, k, core) + index], spread_slot(c, k, i),
+            wid_s.at[c, k, sem], wid_r.at[c, k, sem], {"wid": flipped(crossed)},
+        )
+
+    def spread_slot(c, k, i):
+        return rb3.at[c, k] if i == 2 else rb2.at[c, k, i]
+
+    def spread_gather(c, k, i):
+        ref = ag.at[(c, k, core) + bits]
+        sem = (4, 5, 9)[i]
+        return remote(ref, ref, wid_s.at[c, k, sem], wid_r.at[c, k, sem], {"wid": flipped(spread(k, i))})
+
     def add_into(ref, other):
         ref[...] = (ref[...].astype(F32) + other[...].astype(F32)).astype(BF)
 
@@ -220,32 +269,58 @@
     def step_pair(c, k, s):
         pair_sum(c, k, s).wait_recv()
         add_into(part.at[(c, k, core) + at_bits(ORDER[k][s:])], (rb1, rb2)[s - 1].at[c, k])
-        go(pair_sum(c, k, s + 1))
+        if c in SPREAD:
+            for i in range(3):
+                go(spread_sum(c, k, i))
+        else:
+            go(pair_sum(c, k, s + 1))
 
     def step_nonlinear(c):
         sums = []
         for k in range(3):
-            pair_sum(c, k, 3).wait_recv()
-            sums.append(part[(c, k, core) + bits].astype(F32) + rb3[c, k].astype(F32))
+            total = part[(c, k, core) + bits].astype(F32)
+            if c in SPREAD:
+                for i in range(3):
+                    spread_sum(c, k, i).wait_recv()
+                    total += spread_slot(c, k, i)[...].astype(F32)
+            else:
+                pair_sum(c, k, 3).wait_recv()
+                total += rb3[c, k].astype(F32)
+            sums.append(total)
+
+        def pass_on(k):
+            if c in SPREAD:
+                for i in range(3):
+                    go(spread_gather(c, k, i))
+            else:
+                go(pair_gather(c, k, 3))
+
         gate, upper, grad = sums
         sigma = jax.nn.sigmoid(gate)
         active = gate * sigma
         ag[(c, 1, core) + bits] = (grad * upper * sigma * (1.0 + gate * (1.0 - sigma))).astype(BF)
-        go(pair_gather(c, 1, 3))
+        pass_on(1)
         ag[(c, 2, core) + bits] = (grad * active).astype(BF)
-        go(pair_gather(c, 2, 3))
+        pass_on(2)
         ag[(c, 0, core) + bits] = (active * upper).astype(BF)
-        go(pair_gather(c, 0, 3))
+        pass_on(0)
 
     def step_gather(c, k, s):
-        pair_gather(c, k, s).wait_recv()
+        if c in SPREAD and s == 2:
+            for i in range(3):
+                spread_gather(c, k, i).wait_recv()
+        else:
+            pair_gather(c, k, s).wait_recv()
         go(pair_gather(c, k, s - 1) if s > 1 else core_gather(c, k))
 
     def z_send(block):
         r, xh = block
         c, i = POS[block]
-        hop = way_of(block) % NZ if chained(block) else r
-        return remote(term.at[c, i], zin.at[r, xh], z_s.at[r, xh], z_r.at[r, xh], {"hid": z_peer(hop)})
+        if block in DIRECT:
+            peer = side_peer(r)
+        else:
+            peer = z_peer(way_of(block) % NZ if chained(block) else r)
+        return remote(term.at[c, i], zin.at[r, xh], z_s.at[r, xh], z_r.at[r, xh], {"hid": peer})
 
     landed = set()
 
@@ -271,7 +346,7 @@
     def home_sum(xh):
         total = term[POS[0, xh]].astype(F32)
         for block in HOME:
-            if block[1] == xh:
+            if (0 if block in DIRECT else block[1]) == xh:
                 z_send(block).wait_recv()
                 total += zin[block].astype(F32)
         return total
@@ -394,8 +469,10 @@
             dma((2, 2)),
             dma((2, 4, 2, 2)),
             dma((2, 4, 2, 2)),
-            dma((NC, 3, 8)),
-            dma((NC, 3, 8)),
+            dma((2, 4, 2)),
+            dma((2, 4, 2)),
+            dma((NC, 3, 10)),
+            dma((NC, 3, 10)),
             dma((NZ, 2)),
             dma((NZ, 2)),
             dma((2,)),

time: 89.6 us -> 86.4 us (0.964); the launches traced: 88.5 us -> 86.2 us
  Pallas kernels: 83.8 us -> 81.6 us
    pallas_call x1, Pallas kernels: 83.8 us -> 81.6 us  [body(): pl.pallas_call(kernel, out_shape=tuple((pltpu.VMEM(shape.shape, shape.dty...]
where the time goes in v3:
time: 86.4 us; the launch traced here: 86.2 us
  Pallas kernels  81.6 us (94%)
  local copies, waits for them, and re-layouts  3.99 us (5%)
    pallas_call x1, Pallas kernels, body(): pl.pallas_call(kernel, out_shape=tuple((pltpu.VMEM(shape.shape, shape.dty...  81.6 us
    unnamed x5, local copies, waits for them, and re-layouts  3.99 us

profile of v3, /device:TPU:1, one launch (start us, length us, event | category | flops | bytes accessed | tf_op | source)
XLA Modules:
  0.0 86.2 jit_solution(1998477350828013635)
XLA Ops:
  0.6 81.6 %shard_map.119 = (bf16[64,512]{1,0:T(8,128)(2,1)S(1)}, bf16[512,896]{1,0:T(8,128)(2,1)S(1)}, bf16[512,896]{1,0:T(8,128)(2,1)S(1)}, bf16[896,512]{1,0:T(8,128)(2,1)S(1)}, f32[3,4,7]{2,1,0:T(4,128)S(1)}) custom-call(bf16[64,512]{1,0:T(8,128)(2,1)} %tok_in.1, bf16[64,512]{1,0:T(8,128)(2,1)} %gro_in.1, bf16[512,896]{1,0:T(8,128)(2,1)} %gc_in.1, f32[4,7]{1,0:T(4,128)} %gs.1, ...), custom_call_target="tpu_custom_call" | custom-call | tf_op jit(solution)/shard_map/pallas_call | solution.py:441
  82.2 0.6 copy.18
  82.9 0.6 copy.22
  83.5 0.9 %copy.19 = bf16[512,896]{1,0:T(8,128)(2,1)} copy(bf16[512,896]{1,0:T(8,128)(2,1)S(1)} %get-tuple-element.6) | data formatting | bytes 1835008
  84.4 0.9 %copy.20 = bf16[512,896]{1,0:T(8,128)(2,1)} copy(bf16[512,896]{1,0:T(8,128)(2,1)S(1)} %get-tuple-element.7) | data formatting | bytes 1835008
  85.3 0.9 %copy.21 = bf16[896,512]{1,0:T(8,128)(2,1)} copy(bf16[896,512]{1,0:T(8,128)(2,1)S(1)} %get-tuple-element.8) | data formatting | bytes 1835008

commit v4 on v3

--- a/solution.py
+++ b/solution.py
@@ -420,9 +420,10 @@
         "E": step_last,
     }
     for name, *at in STEPS:
+        if name == "E":
+            for copy in sends:
+                copy.wait_send()
         do[name](*at)
-    for copy in sends:
-        copy.wait_send()
 
 
 def body(tokens, grad_out, gate_codes, gate_scale, up_codes, up_scale, down_codes, down_scale):

time: 86.4 us -> 86.1 us (level)
  no operation moved by 1% of the time
where the time goes in v4:
time: 86.1 us; the launch traced here: 86 us
  Pallas kernels  81.4 us (95%)
  local copies, waits for them, and re-layouts  3.99 us (5%)
    pallas_call x1, Pallas kernels, body(): pl.pallas_call(kernel, out_shape=tuple((pltpu.VMEM(shape.shape, shape.dty...  81.4 us
    unnamed x5, local copies, waits for them, and re-layouts  3.99 us

profile of v4, /device:TPU:1, one launch (start us, length us, event | category | flops | bytes accessed | tf_op | source)
XLA Modules:
  0.0 86.0 jit_solution(3662513508807960085)
XLA Ops:
  0.6 81.4 %shard_map.119 = (bf16[64,512]{1,0:T(8,128)(2,1)S(1)}, bf16[512,896]{1,0:T(8,128)(2,1)S(1)}, bf16[512,896]{1,0:T(8,128)(2,1)S(1)}, bf16[896,512]{1,0:T(8,128)(2,1)S(1)}, f32[3,4,7]{2,1,0:T(4,128)S(1)}) custom-call(bf16[64,512]{1,0:T(8,128)(2,1)} %tok_in.1, bf16[64,512]{1,0:T(8,128)(2,1)} %gro_in.1, bf16[512,896]{1,0:T(8,128)(2,1)} %gc_in.1, f32[4,7]{1,0:T(4,128)} %gs.1, ...), custom_call_target="tpu_custom_call" | custom-call | tf_op jit(solution)/shard_map/pallas_call | solution.py:442
  82.0 0.6 copy.18
  82.6 0.6 copy.22
  83.2 0.9 %copy.19 = bf16[512,896]{1,0:T(8,128)(2,1)} copy(bf16[512,896]{1,0:T(8,128)(2,1)S(1)} %get-tuple-element.6) | data formatting | bytes 1835008
  84.2 0.9 %copy.20 = bf16[512,896]{1,0:T(8,128)(2,1)} copy(bf16[512,896]{1,0:T(8,128)(2,1)S(1)} %get-tuple-element.7) | data formatting | bytes 1835008
  85.1 0.9 %copy.21 = bf16[896,512]{1,0:T(8,128)(2,1)} copy(bf16[896,512]{1,0:T(8,128)(2,1)S(1)} %get-tuple-element.8) | data formatting | bytes 1835008
